TPU v7x, 32 devices: a whole 2x2x4 slice. The times are simulated.
32 devices in a mesh: seq: 4 (over y, core), vocab: 8 (over z, x).
Axes of the slice: x: 2, y: 2, z: 4, core: 2. Of those that a mesh axis runs over, the one named last changes fastest.
Arguments:
- queries: bfloat16 [2048, 2, 2048], P(('seq', 'vocab')), may hold values from -40 to 40
- key_vectors: bfloat16 [2048, 2, 2048], P(('seq', 'vocab')), may hold values from -40 to 40
- value_vectors: bfloat16 [2048, 2, 2048], P(('seq', 'vocab')), may hold values from -18 to 18
- residual: bfloat16 [2048, 2, 2048], P(('seq', 'vocab')), may hold values from -3 to 3
- norm_gain: float32 [2048], replicated, may hold values from 0.1 to 1.9
- head_weight: bfloat16 [2048, 8192], P(None, 'vocab'), may hold values from -0.125 to 0.125
- head_bias: float32 [8192], P('vocab'), may hold values from -6 to 6
- doc_lengths: int32 [2], replicated, may hold values from 1 to 2048, 3072 in all
Outputs:
- pooled: float32 [2, 8192], P(None, 'vocab')
- grad_hidden: bfloat16 [2048, 2, 2048], P(('seq', 'vocab'))
Inputs may be any that keep to these rules, and one draw needn't show every extreme that they name: `doc_lengths`: the lengths add up to 3072.
All inputs are finite; a program needn't handle non-finite values.
Results may differ from a plain program's by a relative error of at most 0.018.
Values may be sent and summed in bfloat16 or wider, within the bound.
A program may use at most 128 MiB of HBM per device.

v0:
```python
import math

import jax
import jax.numpy as jnp
from jax import lax
from jax.sharding import PartitionSpec as P

HEAD_DIM = 128


sharpness = 8.0
flops_weight = 500.0
epsilon = 1e-05


def local(
    queries, key_vectors, value_vectors, residual, norm_gain, head_weight, head_bias, doc_lengths
):
    tokens_here = queries.shape[0]
    docs_count = queries.shape[1]
    vocab_count = lax.axis_size("vocab")
    seq_at = lax.axis_index("seq")
    query_heads, key_heads, value_heads = (
        lax.all_to_all(queries, "seq", split_axis=2, concat_axis=0, tiled=True),
        lax.all_to_all(key_vectors, "seq", split_axis=2, concat_axis=0, tiled=True),
        lax.all_to_all(value_vectors, "seq", split_axis=2, concat_axis=0, tiled=True),
    )
    block_rows = query_heads.shape[0]
    local_width = query_heads.shape[2]
    local_heads = local_width // HEAD_DIM
    query_split = query_heads.reshape(block_rows, docs_count, local_heads, HEAD_DIM)
    within = jnp.arange(block_rows, dtype=jnp.int32)

    def attend_block(carry, block):
        highest, total, summed = carry
        key_block, value_block, shard = block
        key_split = key_block.reshape(block_rows, docs_count, local_heads, HEAD_DIM)
        value_split = value_block.reshape(block_rows, docs_count, local_heads, HEAD_DIM)
        key_place = (
            within // tokens_here * vocab_count + shard
        ) * tokens_here + within % tokens_here
        allowed = (key_place[None, :] < doc_lengths[:, None])[:, None, None, :]
        scores = jnp.einsum(
            "qbhe,kbhe->bhqk", query_split, key_split, preferred_element_type=jnp.float32
        ) / math.sqrt(HEAD_DIM)
        block_top = jnp.max(jnp.where(allowed, scores, -1e30), axis=3)
        new_top = jnp.maximum(highest, block_top)
        weights = jnp.where(allowed, jnp.exp(scores - new_top[..., None]), 0.0)
        shrink = jnp.exp(highest - new_top)
        total = total * shrink + jnp.sum(weights, axis=3)
        added = jnp.einsum(
            "bhqk,kbhe->qbhe",
            weights.astype(jnp.bfloat16),
            value_split,
            preferred_element_type=jnp.float32,
        )
        summed = summed * jnp.transpose(shrink, (2, 0, 1))[..., None] + added
        return ((new_top, total, summed), None)

    initial = (
        jnp.full((docs_count, local_heads, block_rows), -1e30, jnp.float32),
        jnp.zeros((docs_count, local_heads, block_rows), jnp.float32),
        jnp.zeros((block_rows, docs_count, local_heads, HEAD_DIM), jnp.float32),
    )
    carry = initial
    key_piece = lax.all_gather(key_heads, "vocab", axis=0, tiled=True)
    value_piece = lax.all_gather(value_heads, "vocab", axis=0, tiled=True)
    count = key_piece.shape[0] // block_rows
    key_blocks = key_piece.reshape(count, block_rows, docs_count, local_width)
    value_blocks = value_piece.reshape(count, block_rows, docs_count, local_width)
    shards = jnp.arange(count, dtype=jnp.int32)
    carry, unused = lax.scan(attend_block, carry, (key_blocks, value_blocks, shards))
    highest, total, summed = carry
    attended = (
        (summed / jnp.transpose(total, (2, 0, 1))[..., None])
        .reshape(block_rows, docs_count, local_width)
        .astype(jnp.bfloat16)
    )
    returned = lax.all_to_all(attended, "seq", split_axis=0, concat_axis=2, tiled=True)
    combined = residual.astype(jnp.float32) + returned.astype(jnp.float32)
    inv_rms = lax.rsqrt(jnp.mean(combined * combined, axis=2, keepdims=True) + epsilon)
    hidden = (combined * inv_rms * norm_gain).astype(jnp.bfloat16)
    arrived = lax.all_gather(hidden, "vocab", axis=0, tiled=True)
    row_count = arrived.shape[0]
    flattened = jnp.dot(
        arrived.reshape(row_count * docs_count, arrived.shape[2]),
        head_weight,
        preferred_element_type=jnp.float32,
    )
    logits = flattened.reshape(row_count, docs_count, head_weight.shape[1]) + head_bias
    gathered_rows = logits.shape[0]
    row_index = jnp.arange(gathered_rows, dtype=jnp.int32)
    position = (
        seq_at * vocab_count + row_index // tokens_here
    ) * tokens_here + row_index % tokens_here
    row_allowed = position[:, None] < doc_lengths[None, :]
    saturated = jnp.log1p(jnp.maximum(logits, 0.0))
    boosted = jnp.where(row_allowed[:, :, None], jnp.exp(sharpness * saturated), 0.0)
    partial_sums = jnp.sum(boosted, axis=0)
    lengths_float = doc_lengths[:, None].astype(jnp.float32)
    totals = lax.psum(partial_sums, "seq")
    pooled = jnp.log(totals / lengths_float) / sharpness
    coefficient = 2.0 * flops_weight / docs_count * jnp.mean(pooled, axis=0)[None, :] / totals
    derivative = jnp.where(logits > 0.0, 1.0 / (1.0 + jnp.maximum(logits, 0.0)), 0.0)
    dlogits = (coefficient[None, :, :] * boosted * derivative).astype(jnp.bfloat16)
    flattened = lax.dot_general(
        dlogits.reshape(gathered_rows * docs_count, dlogits.shape[2]),
        head_weight,
        (((1,), (1,)), ((), ())),
        preferred_element_type=jnp.float32,
    )
    own_rows = lax.psum_scatter(
        flattened.reshape(gathered_rows, docs_count, head_weight.shape[0]).astype(jnp.bfloat16),
        "vocab",
        scatter_dimension=0,
        tiled=True,
    )
    return (pooled, own_rows)


def solution(mesh):
    in_specs = (
        P(("seq", "vocab"), None, None),
        P(("seq", "vocab"), None, None),
        P(("seq", "vocab"), None, None),
        P(("seq", "vocab"), None, None),
        P(),
        P(None, "vocab"),
        P("vocab"),
        P(),
    )
    out_specs = (P(None, "vocab"), P(("seq", "vocab"), None, None))
    return jax.shard_map(local, mesh=mesh, in_specs=in_specs, out_specs=out_specs, check_vma=False)
```

profile of v0, /device:TPU:0, one launch (start us, length us, event | category | flops | bytes accessed | tf_op | source)
XLA Modules:
  0.0 451.0 jit_solution(4301750633245682184)
XLA Ops:
  7.2 2.6 copy.70
  9.9 0.9 reshape.208
  10.7 12.9 %all_to_all.60 = bf16[4,2,32768]{2,1,0:T(2,128)(2,1)S(1)} all-to-all(bf16[4,2,32768]{2,1,0:T(2,128)(2,1)S(1)} %reshape.208), channel_id=1, replica_groups=mesh['seq'=4,'vocab'=8] {'seq'}, dimensions={0} | all-to-all | bytes 1048576 | tf_op jit(solution)/shard_map/all_to_all | solution.py:25
  23.6 0.7 reshape.209
  24.3 0.9 copy.87
  25.2 0.9 copy.72
  26.2 0.9 copy.75
  27.1 0.9 reshape.212
  28.0 11.2 %all_to_all.61 = bf16[4,2,32768]{2,1,0:T(2,128)(2,1)S(1)} all-to-all(bf16[4,2,32768]{2,1,0:T(2,128)(2,1)S(1)} %reshape.212), channel_id=1, replica_groups=mesh['seq'=4,'vocab'=8] {'seq'}, dimensions={0} | all-to-all | bytes 1048576 | tf_op jit(solution)/shard_map/all_to_all | solution.py:26
  39.2 0.7 reshape.213
  40.0 0.9 copy.88
  40.8 0.9 copy.77
  41.8 0.9 copy.73
  42.7 1.6 reshape.210
  44.2 3.5 all-to-all-start.1
  47.8 8.7 %all-to-all-done.1 = bf16[4,2,32768]{2,1,0:T(2,128)(2,1)S(1)} async-done(((bf16[4,2,32768]{2,1,0:T(2,128)(2,1)}), bf16[4,2,32768]{2,1,0:T(2,128)(2,1)S(1)}, u32[]{:S(2)}, u32[]{:S(2)}) %all-to-all-start.1) | async-done | bytes 524320 | tf_op jit(solution)/shard_map/all_to_all | solution.py:24
  56.5 0.7 reshape.211
  57.3 0.7 copy.74
  58.1 0.9 copy.79
  59.0 41.0 %all-gather.4.cloned.1.call-done = bf16[2048,2,512]{2,0,1:T(8,128)(2,1)} async-done(((bf16[256,2,512]{2,0,1:T(8,128)(2,1)}), bf16[2048,2,512]{2,0,1:T(8,128)(2,1)}) %all-gather.4.cloned.1.call-update) | async-done | bytes 4194320 | tf_op jit(solution)/shard_map/all_gather | solution.py:66
  100.0 73.9 %all-gather.6.cloned.1.call-done = bf16[2048,2,512]{2,0,1:T(8,128)(2,1)} async-done(((bf16[256,2,512]{2,0,1:T(8,128)(2,1)}), bf16[2048,2,512]{2,0,1:T(8,128)(2,1)}) %all-gather.6.cloned.1.call-update) | async-done | bytes 4194320 | tf_op jit(solution)/shard_map/all_gather | solution.py:67
  173.8 63.2 %while.20 = (s32[]{:T(128)}, f32[2,4,256]{2,1,0:T(4,128)S(1)}, f32[2,4,256]{2,1,0:T(4,128)S(1)}, f32[256,2,4,128]{0,3,2,1:T(8,128)}, s32[8]{0:T(128)S(1)}, /*ind...) while((s32[]{:T(128)}, f32[2,4,256]{2,1,0:T(4,128)S(1)}, ...), condition=%wide.region_3.4_spmd.clone.clone, body=%wide.region_0.3_spmd.clone.clone.sunk | while | flops 275005952 | bytes 14291605 | solution.py:72
  174.5 0.7 fusion.69
  175.2 1.3 constant_dynamic-slice_fusion.3
  176.7 1.6 select_reduce_fusion.2
  178.5 1.7 fusion.72
  181.3 0.7 fusion.69
  182.0 1.3 constant_dynamic-slice_fusion.3
  183.5 1.6 select_reduce_fusion.2
  185.3 2.9 fusion.72
  189.3 0.7 fusion.69
  190.1 1.3 constant_dynamic-slice_fusion.3
  191.5 1.6 select_reduce_fusion.2
  193.4 2.9 fusion.72
  197.4 0.7 fusion.69
  198.1 1.3 constant_dynamic-slice_fusion.3
  199.6 1.6 select_reduce_fusion.2
  201.4 2.9 fusion.72
  205.4 0.7 fusion.69
  206.2 1.3 constant_dynamic-slice_fusion.3
  207.7 1.6 select_reduce_fusion.2
  209.5 2.9 fusion.72
  213.5 0.7 fusion.69
  214.2 1.3 constant_dynamic-slice_fusion.3
  215.7 1.6 select_reduce_fusion.2
  217.5 2.9 fusion.72
  221.5 0.7 fusion.69
  222.3 1.3 constant_dynamic-slice_fusion.3
  223.8 1.6 select_reduce_fusion.2
  225.6 2.9 fusion.72
  230.3 1.3 constant_dynamic-slice_fusion.3
  231.8 1.6 select_reduce_fusion.2
  233.6 2.9 fusion.72
  237.0 1.4 divide_convert_fusion
  238.9 11.4 %all_to_all.62 = bf16[256,2,512]{2,1,0:T(2,128)(2,1)S(1)} all-to-all(bf16[256,2,512]{2,1,0:T(2,128)(2,1)S(1)} %copy.89), channel_id=1, replica_groups=mesh['seq'=4,'vocab'=8] {'seq'}, dimensions={0} | all-to-all | bytes 1048576 | tf_op jit(solution)/shard_map/all_to_all | solution.py:79
  250.9 1.1 multiply_convert_fusion.2
  252.4 70.6 %all-gather.8.cloned.1.call-done = bf16[512,2,2048]{2,0,1:T(8,128)(2,1)} async-done(((bf16[64,2,2048]{2,0,1:T(8,128)(2,1)}), bf16[512,2,2048]{2,0,1:T(8,128)(2,1)}) %all-gather.8.cloned.1.call-update) | async-done | bytes 4194320 | tf_op jit(solution)/shard_map/all_gather | solution.py:83
  322.9 11.4 %fusion.27 = (f32[2,1024]{1,0:T(2,128)S(1)}, f32[512,2,1024]{2,0,1:T(8,128)}) fusion(f32[1024]{0:T(1024)S(1)} %copy-done.6, pred[512,2]{0,1:T(4,128)(4,1)S(1)} %broadcast_compare_fusion.1, bf16[512,2,2048]{2,0,1:T(8,128)(2,1)} %all-gather.8.cloned.1.call-done, bf16[2048,1024]{1,0:T(8,128)(2,1)} %param.15), kind=kOutput, calls=%fused_computation.44 | convolution fusion | flops 4300208128 | bytes 12596224 | tf_op jit(solution)/shard_map/dot_general | solution.py:85
  334.3 5.7 %psum.7 = f32[2,1024]{1,0:T(2,128)S(1)} all-reduce(f32[2,1024]{1,0:T(2,128)S(1)} %get-tuple-element.387), channel_id=1, replica_groups=mesh['seq'=4,'vocab'=8] {'seq'}, use_global_device_ids=true, to_apply=%region_6.7 | all-reduce | flops 2048 | bytes 16384 | tf_op jit(solution)/shard_map/psum | solution.py:101
  340.1 0.7 fusion.54
  340.8 3.3 fusion.38
  344.1 11.1 %fusion.28 = bf16[512,2,2048]{2,0,1:T(8,128)(2,1)} fusion(bf16[2048,1024]{1,0:T(8,128)(2,1)} %param.15, f32[512,2,1024]{2,0,1:T(8,128)S(1)} %copy-done, f32[2,1024]{1,0:T(2,128)S(1)} %broadcast_divide_fusion, f32[1024]{0:T(1024)S(1)} %copy-done.6, pred[512,2]{0,1:T(4,128)(4,1)S(1)} %broadcast_compare_fusion.1, u8[512,1024]{1,0:T(8,128)(4,1)S(1)} %fusion.38), kind=kOutput, calls=%fused_computation.45 | convolution fusion | flops 4311744512 | bytes 13120512 | tf_op jit(solution)/shard_map/dot_general | solution.py:106
  355.2 86.8 %reduce-scatter.2.cloned.1.call-done = bf16[64,2,2048]{2,0,1:T(8,128)(2,1)} async-done(((bf16[512,2,2048]{2,0,1:T(8,128)(2,1)}), bf16[64,2,2048]{2,0,1:T(8,128)(2,1)}) %reduce-scatter.2.cloned.1.call-update) | async-done | bytes 524304 | tf_op jit(solution)/shard_map/reduce_scatter | solution.py:112
  442.1 2.4 copy.84
  (111 shorter events, 15.1 us)
Async XLA Ops:
  7.2 19.1 %copy-start.2 = (bf16[64,2,2048]{2,1,0:T(2,128)(2,1)S(1)}, bf16[64,2,2048]{2,1,0:T(2,128)(2,1)}, u32[]{:S(2)}) copy-start(bf16[64,2,2048]{2,1,0:T(2,128)(2,1)} %param.12) | copy-start | bytes 1572868
  7.2 92.8 %all-gather.4.cloned.1.call-start = ((), (), s32[]{:S(2)}) async-start(), calls=%async_computation.5 | async-start | bytes 4718592 | tf_op jit(solution)/shard_map/all_gather | solution.py:66
  26.2 15.6 %copy-start.3 = (bf16[64,2,2048]{2,1,0:T(2,128)(2,1)S(1)}, bf16[64,2,2048]{2,1,0:T(2,128)(2,1)}, u32[]{:S(2)}) copy-start(bf16[64,2,2048]{2,1,0:T(2,128)(2,1)} %param.10) | copy-start | bytes 1572868
  26.2 147.7 %all-gather.6.cloned.1.call-start = ((), (), s32[]{:S(2)}) async-start(), calls=%async_computation.6 | async-start | bytes 4718592 | tf_op jit(solution)/shard_map/all_gather | solution.py:67
  42.7 131.2 %copy-start.4 = (s32[2]{0:T(128)S(1)}, s32[2]{0:T(128)}, u32[]{:S(2)}) copy-start(s32[2]{0:T(128)} %param.17) | copy-start | bytes 28
  44.2 12.3 %all-to-all-start.1 = ((bf16[4,2,32768]{2,1,0:T(2,128)(2,1)}), bf16[4,2,32768]{2,1,0:T(2,128)(2,1)S(1)}, u32[]{:S(2)}, u32[]{:S(2)}) async-start(bf16[4,2,32768]{2,1,0:T(2,128)(2,1)} %reshape.210), calls=%async_computation.1 | async-start | bytes 1048576 | tf_op jit(solution)/shard_map/all_to_all | solution.py:24
  47.7 275.2 %all-gather.8.cloned.1.call-start = ((), (), s32[]{:S(2)}) async-start(), calls=%async_computation.7 | async-start | bytes 4718592 | tf_op jit(solution)/shard_map/all_gather | solution.py:83
  237.0 13.6 %copy-start.1 = (bf16[64,2,2048]{2,1,0:T(2,128)(2,1)S(1)}, bf16[64,2,2048]{2,1,0:T(2,128)(2,1)}, u32[]{:S(2)}) copy-start(bf16[64,2,2048]{2,1,0:T(2,128)(2,1)} %param.13) | copy-start | bytes 1572868
  238.4 12.5 %copy-start.5 = (f32[2048]{0:T(1024)S(1)}, f32[2048]{0:T(1024)}, u32[]{:S(2)}) copy-start(f32[2048]{0:T(1024)} %param.14) | copy-start | bytes 24580
  250.4 72.5 %copy-start.6 = (f32[1024]{0:T(1024)S(1)}, f32[1024]{0:T(1024)}, u32[]{:S(2)}) copy-start(f32[1024]{0:T(1024)} %param.16) | copy-start | bytes 12292
  252.0 190.0 %reduce-scatter.2.cloned.1.call-start = ((), (), s32[]{:S(2)}) async-start(), calls=%async_computation.8 | async-start | bytes 4718592 | tf_op jit(solution)/shard_map/reduce_scatter | solution.py:112
  340.1 4.0 copy-start
Sparse Core Ops, SparseCore 0:
  26.3 73.6 all-gather.3
  102.2 71.6 all-gather.5
  252.1 70.7 all-gather.7
  355.4 86.6 reduce-scatter.1
where the time goes:
time: 452 us; the launch traced here: 451 us
  waiting for transfers between devices  281 us (62%)
  matrix products  57.1 us (13%)
  blocking collectives  41.3 us (9%)
  local copies, waits for them, and re-layouts  36.3 us (8%)
  other arithmetic  16.9 us (4%)
  between operations  14.1 us (3%)
    reduce_scatter x1, waiting for transfers between devices, local(): lax.psum_scatter(flattened.reshape(gathered_rows, docs_count, head_weight...  86.8 us
    all_gather x1, waiting for transfers between devices, local(): value_piece = lax.all_gather(value_heads, 'vocab', axis=0, tiled=True)  73.9 us
    all_gather x1, waiting for transfers between devices, local(): arrived = lax.all_gather(hidden, 'vocab', axis=0, tiled=True)  70.6 us
    all_gather x1, waiting for transfers between devices, local(): key_piece = lax.all_gather(key_heads, 'vocab', axis=0, tiled=True)  41 us
    dot_general x8, matrix products, attend_block(): jnp.einsum('bhqk,kbhe->qbhe', weights.astype(jnp.bfloat16), value_split,...  21.8 us
    dynamic_slice x32, local copies, waits for them, and re-layouts, local(): lax.scan(attend_block, carry, (key_blocks, value_blocks, shards))  18.1 us
    unnamed x25, local copies, waits for them, and re-layouts  13.1 us
    all_to_all x1, blocking collectives, local(): lax.all_to_all(key_vectors, 'seq', split_axis=2, concat_axis=0, tiled=True)  12.9 us
  transfers between devices with their start and end apart: 5, of which 5 were waited for; matrix products, arithmetic and copies ran while one was open for 2% of the time, Pallas kernels for 0%

commit v1 on v0

--- a/solution.py
+++ b/solution.py
@@ -1,8 +1,11 @@
+import functools
 import math
 
 import jax
 import jax.numpy as jnp
 from jax import lax
+from jax.experimental import pallas as pl
+from jax.experimental.pallas import tpu as pltpu
 from jax.sharding import PartitionSpec as P
 
 HEAD_DIM = 128
@@ -13,13 +16,185 @@
 epsilon = 1e-05
 
 
-def local(
-    queries, key_vectors, value_vectors, residual, norm_gain, head_weight, head_bias, doc_lengths
+def place(device, vocab_count):
+    return (device // vocab_count, device % vocab_count)
+
+
+def meet(devices, me, vocab_count):
+    barrier = pltpu.get_barrier_semaphore()
+
+    @pl.loop(1, devices)
+    def greet(step):
+        pl.semaphore_signal(
+            barrier,
+            inc=1,
+            device_id=place((me + step) % devices, vocab_count),
+            device_id_type=pl.DeviceIdType.MESH,
+        )
+
+    pl.semaphore_wait(barrier, devices - 1)
+
+
+def attend_kernel(
+    devices,
+    vocab_count,
+    heads,
+    chunk_blocks,
+    lengths_ref,
+    packed_ref,
+    residual_ref,
+    gain_ref,
+    hidden_ref,
+    arrived,
+    attended,
+    returned,
+    send_sem,
+    recv_sem,
+    back_send_sem,
+    back_recv_sem,
+    own_sem,
+):
+    me = lax.axis_index("seq") * vocab_count + lax.axis_index("vocab")
+    docs_count, tokens_here, _ = hidden_ref.shape
+    chunk = chunk_blocks * tokens_here
+    length = devices * tokens_here
+    meet(devices, me, vocab_count)
+
+    def outgoing(other, source):
+        return pltpu.make_async_remote_copy(
+            src_ref=packed_ref.at[other],
+            dst_ref=arrived.at[source],
+            send_sem=send_sem.at[other],
+            recv_sem=recv_sem.at[source],
+            device_id=place(other, vocab_count),
+            device_id_type=pl.DeviceIdType.MESH,
+        )
+
+    def back(other, source):
+        return pltpu.make_async_remote_copy(
+            src_ref=attended.at[other],
+            dst_ref=returned.at[source],
+            send_sem=back_send_sem.at[other],
+            recv_sem=back_recv_sem.at[source],
+            device_id=place(other, vocab_count),
+            device_id_type=pl.DeviceIdType.MESH,
+        )
+
+    @pl.loop(1, devices)
+    def send(step):
+        outgoing((me + step) % devices, me).start()
+
+    own = pltpu.make_async_copy(packed_ref.at[me], arrived.at[me], own_sem)
+    own.start()
+    own.wait()
+
+    @pl.loop(1, devices)
+    def receive(step):
+        other = (me + step) % devices
+        outgoing(other, other).wait_recv()
+
+    real = lengths_ref[me // heads]
+    slots = lax.broadcasted_iota(jnp.int32, (1, length), 1)
+    bias = jnp.where(slots < real, 0.0, -1e30)
+    factor = math.log2(math.e) / math.sqrt(HEAD_DIM)
+    count = devices // chunk_blocks
+
+    @pl.loop(0, count)
+    def attend(step):
+        first = ((step + me // chunk_blocks) % count) * chunk_blocks
+        query = arrived[pl.ds(first, chunk_blocks), 0].reshape(chunk, HEAD_DIM)
+        keys = arrived[:, 1].reshape(length, HEAD_DIM)
+        scores = lax.dot_general(
+            query, keys, (((1,), (1,)), ((), ())), preferred_element_type=jnp.float32
+        )
+        scores = scores + bias
+        top = jnp.max(scores, axis=1, keepdims=True)
+        weights = jnp.exp2((scores - top) * factor)
+        total = jnp.sum(weights, axis=1, keepdims=True)
+        values = arrived[:, 2].reshape(length, HEAD_DIM)
+        summed = jnp.dot(
+            weights.astype(jnp.bfloat16), values, preferred_element_type=jnp.float32
+        )
+        result = (summed / total).astype(jnp.bfloat16)
+        attended[pl.ds(first, chunk_blocks)] = result.reshape(
+            chunk_blocks, tokens_here, HEAD_DIM
+        )
+        for block in range(chunk_blocks):
+            other = first + block
+
+            @pl.when(other != me)
+            def give():
+                back(other, me).start()
+
+    keep = pltpu.make_async_copy(attended.at[me], returned.at[me], own_sem)
+    keep.start()
+    keep.wait()
+
+    @pl.loop(1, devices)
+    def finish(step):
+        other = (me + step) % devices
+        back(other, other).wait_recv()
+
+    for doc in range(docs_count):
+        combined = []
+        squares = jnp.zeros((tokens_here, HEAD_DIM), jnp.float32)
+        for head in range(heads):
+            term = residual_ref[doc, :, head * HEAD_DIM : (head + 1) * HEAD_DIM].astype(
+                jnp.float32
+            ) + returned[doc * heads + head].astype(jnp.float32)
+            squares = squares + term * term
+            combined.append(term)
+        mean = jnp.sum(squares, axis=1, keepdims=True) / (heads * HEAD_DIM)
+        inv_rms = lax.rsqrt(mean + epsilon)
+        for head in range(heads):
+            at = slice(head * HEAD_DIM, (head + 1) * HEAD_DIM)
+            hidden_ref[doc, :, at] = (combined[head] * inv_rms * gain_ref[:, at]).astype(
+                jnp.bfloat16
+            )
+
+    @pl.loop(1, devices)
+    def drain(step):
+        other = (me + step) % devices
+        outgoing(other, me).wait_send()
+        back(other, me).wait_send()
+
+
+def attend_all(queries, key_vectors, value_vectors, residual, norm_gain, doc_lengths):
+    tokens_here, docs_count, width = queries.shape
+    heads = width // HEAD_DIM
+    vocab_count = lax.axis_size("vocab")
+    devices = lax.axis_size("seq") * vocab_count
+    packed = jnp.stack([queries, key_vectors, value_vectors])
+    packed = packed.reshape(3, tokens_here, docs_count, heads, HEAD_DIM)
+    packed = packed.transpose(2, 3, 0, 1, 4).reshape(devices, 3, tokens_here, HEAD_DIM)
+    vmem = pl.BlockSpec(memory_space=pltpu.VMEM)
+    return pl.pallas_call(
+        functools.partial(attend_kernel, devices, vocab_count, heads, 4),
+        out_shape=jax.ShapeDtypeStruct((docs_count, tokens_here, width), jnp.bfloat16),
+        in_specs=[pl.BlockSpec(memory_space=pltpu.SMEM), vmem, vmem, vmem],
+        out_specs=vmem,
+        scratch_shapes=[
+            pltpu.VMEM((devices, 3, tokens_here, HEAD_DIM), jnp.bfloat16),
+            pltpu.VMEM((devices, tokens_here, HEAD_DIM), jnp.bfloat16),
+            pltpu.VMEM((devices, tokens_here, HEAD_DIM), jnp.bfloat16),
+            pltpu.SemaphoreType.DMA((devices,)),
+            pltpu.SemaphoreType.DMA((devices,)),
+            pltpu.SemaphoreType.DMA((devices,)),
+            pltpu.SemaphoreType.DMA((devices,)),
+            pltpu.SemaphoreType.DMA,
+        ],
+        compiler_params=pltpu.CompilerParams(
+            collective_id=1, has_side_effects=True, vmem_limit_bytes=40 * 1024 * 1024
+        ),
+    )(doc_lengths, packed, residual.transpose(1, 0, 2), norm_gain[None, :])
+
+
+def attend_blocks(
+    queries, key_vectors, value_vectors, residual, norm_gain, doc_lengths
 ):
     tokens_here = queries.shape[0]
     docs_count = queries.shape[1]
     vocab_count = lax.axis_size("vocab")
-    seq_at = lax.axis_index("seq")
     query_heads, key_heads, value_heads = (
         lax.all_to_all(queries, "seq", split_axis=2, concat_axis=0, tiled=True),
         lax.all_to_all(key_vectors, "seq", split_axis=2, concat_axis=0, tiled=True),
@@ -80,6 +255,24 @@
     combined = residual.astype(jnp.float32) + returned.astype(jnp.float32)
     inv_rms = lax.rsqrt(jnp.mean(combined * combined, axis=2, keepdims=True) + epsilon)
     hidden = (combined * inv_rms * norm_gain).astype(jnp.bfloat16)
+    return hidden
+
+
+def local(
+    queries, key_vectors, value_vectors, residual, norm_gain, head_weight, head_bias, doc_lengths
+):
+    tokens_here = queries.shape[0]
+    docs_count = queries.shape[1]
+    vocab_count = lax.axis_size("vocab")
+    seq_at = lax.axis_index("seq")
+    if lax.axis_size("seq") * vocab_count == docs_count * (queries.shape[2] // HEAD_DIM):
+        hidden = attend_all(
+            queries, key_vectors, value_vectors, residual, norm_gain, doc_lengths
+        ).transpose(1, 0, 2)
+    else:
+        hidden = attend_blocks(
+            queries, key_vectors, value_vectors, residual, norm_gain, doc_lengths
+        )
     arrived = lax.all_gather(hidden, "vocab", axis=0, tiled=True)
     row_count = arrived.shape[0]
     flattened = jnp.dot(

time: 452 us -> 273 us (0.60)
  waiting for transfers between devices: 281 us -> 159 us
  Pallas kernels: 0 us -> 60.9 us
  blocking collectives: 41.3 us -> 5.92 us
  matrix products: 57.1 us -> 22.5 us
  local copies, waits for them, and re-layouts: 36.3 us -> 6.35 us
  other arithmetic: 16.9 us -> 4.22 us
    all_gather x2 -> x0, waiting for transfers between devices: 115 us -> none  [the longest x1 73.9 us: local(): value_piece = lax.all_gather(value_heads, 'vocab', axis=0, tiled=True)]
    pallas_call x0 -> x1, Pallas kernels: none -> 60.9 us  [attend_all(): pl.pallas_call(functools.partial(attend_kernel, devices, vocab_count, hea...]
    all_to_all x3 -> x0, blocking collectives: 35.5 us -> none  [the longest x1 12.9 us: local(): lax.all_to_all(key_vectors, 'seq', split_axis=2, concat_axis=0, tiled=True)]
    dot_general x16 -> x0, matrix products: 34.6 us -> none  [the longest x8 21.8 us: attend_block(): jnp.einsum('bhqk,kbhe->qbhe', weights.astype(jnp.bfloat16), value_split,...]
    dynamic_slice x32 -> x0, local copies, waits for them, and re-layouts: 18.1 us -> none  [local(): lax.scan(attend_block, carry, (key_blocks, value_blocks, shards))]
    unnamed x25 -> x14, local copies, waits for them, and re-layouts: 13.1 us -> 2.56 us
    all_to_all x1 -> x0, waiting for transfers between devices: 8.73 us -> none  [local(): lax.all_to_all(queries, 'seq', split_axis=2, concat_axis=0, tiled=True)]
    add x16 -> x0, other arithmetic: 5.38 us -> none  [the longest x8 5.23 us: attend_block(): (within // tokens_here * vocab_count + shard) * tokens_here]
  transfers between devices with their start and end apart: 5 -> 2, of which waited for: 5 -> 2; matrix products, arithmetic and copies ran while one was open for 2% -> 0% of each run, Pallas kernels for 0% -> 0%
where the time goes in v1:
time: 273 us
  waiting for transfers between devices  159 us (58%)
  Pallas kernels  60.9 us (22%)
  matrix products  22.5 us (8%)
  between operations  14.2 us (5%)
  local copies, waits for them, and re-layouts  6.35 us (2%)
  blocking collectives  5.92 us (2%)
  other arithmetic  4.22 us (2%)
    reduce_scatter x1, waiting for transfers between devices, local(): lax.psum_scatter(flattened.reshape(gathered_rows, docs_count, head_weight...  86.6 us
    all_gather x1, waiting for transfers between devices, local(): arrived = lax.all_gather(hidden, 'vocab', axis=0, tiled=True)  72.1 us
    pallas_call x1, Pallas kernels, attend_all(): pl.pallas_call(functools.partial(attend_kernel, devices, vocab_count, hea...  60.9 us
    dot_general x1, matrix products, local(): jnp.dot(arrived.reshape(row_count * docs_count, arrived.shape[2]), head_w...  11.4 us
    dot_general x1, matrix products, local(): lax.dot_general(dlogits.reshape(gathered_rows * docs_count, dlogits.shape...  11.1 us
    psum x1, blocking collectives, local(): totals = lax.psum(partial_sums, 'seq')  5.92 us
  transfers between devices with their start and end apart: 2, of which 2 were waited for; matrix products, arithmetic and copies ran while one was open for 0% of the time, Pallas kernels for 0%

profile of v1, /device:TPU:0, one launch (start us, length us, event | category | flops | bytes accessed | tf_op | source)
XLA Modules:
  0.0 273.0 jit_solution(18029493130713685906)
XLA Ops:
  7.2 0.0 copy-start.3
  7.2 0.0 copy-start.4
  7.2 0.0 all-gather.2.cloned.1.call-start
  7.2 1.5 stack.12
  8.7 0.2 copy.10
  8.9 0.0 copy-start
  8.9 0.0 copy-start.1
  8.9 1.4 stack.13
  10.3 0.2 copy.11
  10.5 0.0 copy-done.3
  10.5 0.3 stack.14
  10.9 0.0 copy-start.5
  10.9 0.2 copy.12
  11.1 0.0 copy-done.4
  11.1 0.2 copy.16
  11.3 0.2 pad_maximum_fusion
  11.5 0.0 copy-done
  11.5 0.0 copy-done.1
  11.5 60.9 %shard_map.95 = bf16[2,64,2048]{2,1,0:T(8,128)(2,1)} custom-call(s32[2]{0:T(128)S(1)} %copy-done.1, bf16[32,3,64,128]{3,2,1,0:T(8,128)(2,1)S(1)} %bitcast.18, bf16[2,64,2048]{2,1,0:T(8,128)(2,1)S(1)} %bitcast.19, f32[1,2048]{1,0:T(1,128)S(1)} %bitcast.20), custom_call_target="tpu_custom_call" | custom-call | tf_op jit(solution)/shard_map/pallas_call | solution.py:171
  72.4 0.0 all-gather.2.cloned.1.call-update
  72.4 0.0 reduce-scatter.2.cloned.1.call-start
  72.5 0.1 broadcast_compare_fusion
  72.6 72.1 %all-gather.2.cloned.1.call-done = bf16[512,2,2048]{2,0,1:T(8,128)(2,1)} async-done(((bf16[64,2,2048]{2,0,1:T(8,128)(2,1)}), bf16[512,2,2048]{2,0,1:T(8,128)(2,1)}) %all-gather.2.cloned.1.call-update) | async-done | bytes 4194320 | tf_op jit(solution)/shard_map/all_gather | solution.py:276
  144.7 0.0 copy-done.5
  144.7 11.4 %fusion.4 = (f32[2,1024]{1,0:T(2,128)S(1)}, f32[512,2,1024]{2,0,1:T(8,128)}) fusion(f32[1024]{0:T(1024)S(1)} %copy-done.5, pred[512,2]{0,1:T(4,128)(4,1)S(1)} %broadcast_compare_fusion, bf16[512,2,2048]{2,0,1:T(8,128)(2,1)} %all-gather.2.cloned.1.call-done, bf16[2048,1024]{1,0:T(8,128)(2,1)} %param.13), kind=kOutput, calls=%fused_computation.8 | convolution fusion | flops 4300208128 | bytes 12596224 | tf_op jit(solution)/shard_map/dot_general | solution.py:278
  156.1 5.9 %psum.7 = f32[2,1024]{1,0:T(2,128)S(1)} all-reduce(f32[2,1024]{1,0:T(2,128)S(1)} %get-tuple-element.6), channel_id=1, replica_groups=mesh['seq'=4,'vocab'=8] {'seq'}, use_global_device_ids=true, to_apply=%region_1.2 | all-reduce | flops 2048 | bytes 16384 | tf_op jit(solution)/shard_map/psum | solution.py:294
  162.0 0.0 copy-start.2
  162.1 0.7 fusion.31
  162.8 3.3 %fusion.15 = u8[512,1024]{1,0:T(8,128)(4,1)S(1)} fusion(f32[512,2,1024]{2,0,1:T(8,128)} %get-tuple-element.7, f32[1024]{0:T(1024)S(1)} %copy-done.5), kind=kLoop, calls=%fused_computation.18 | loop fusion | flops 5767168 | bytes 4722688
  166.0 0.0 copy-done.2
  166.0 11.1 %fusion.5 = bf16[512,2,2048]{2,0,1:T(8,128)(2,1)} fusion(bf16[2048,1024]{1,0:T(8,128)(2,1)} %param.13, f32[512,2,1024]{2,0,1:T(8,128)S(1)} %copy-done.2, f32[2,1024]{1,0:T(2,128)S(1)} %broadcast_divide_fusion, f32[1024]{0:T(1024)S(1)} %copy-done.5, pred[512,2]{0,1:T(4,128)(4,1)S(1)} %broadcast_compare_fusion, u8[512,1024]{1,0:T(8,128)(4,1)S(1)} %fusion.15), kind=kOutput, calls=%fused_computation.9 | convolution fusion | flops 4311744512 | bytes 13120512 | tf_op jit(solution)/shard_map/dot_general | solution.py:299
  177.1 0.0 reduce-scatter.2.cloned.1.call-update
  177.2 86.6 %reduce-scatter.2.cloned.1.call-done = bf16[64,2,2048]{2,0,1:T(8,128)(2,1)} async-done(((bf16[512,2,2048]{2,0,1:T(8,128)(2,1)}), bf16[64,2,2048]{2,0,1:T(8,128)(2,1)}) %reduce-scatter.2.cloned.1.call-update) | async-done | bytes 524304 | tf_op jit(solution)/shard_map/reduce_scatter | solution.py:305
  263.8 2.4 copy.14
  (4 shorter events, 0.0 us)
Async XLA Ops:
  7.2 3.4 %copy-start.3 = (bf16[64,2,2048]{2,1,0:T(2,128)(2,1)S(1)}, bf16[64,2,2048]{2,1,0:T(2,128)(2,1)}, u32[]{:S(2)}) copy-start(bf16[64,2,2048]{2,1,0:T(2,128)(2,1)} %param.10) | copy-start | bytes 1572868
  7.2 3.9 %copy-start.4 = (bf16[64,2,2048]{2,1,0:T(2,128)(2,1)S(1)}, bf16[64,2,2048]{2,1,0:T(2,128)(2,1)}, u32[]{:S(2)}) copy-start(bf16[64,2,2048]{2,1,0:T(2,128)(2,1)} %param.11) | copy-start | bytes 1572868
  7.2 137.5 %all-gather.2.cloned.1.call-start = ((), (), s32[]{:S(2)}) async-start(), calls=%async_computation.1 | async-start | bytes 4718592 | tf_op jit(solution)/shard_map/all_gather | solution.py:276
  8.9 2.6 copy-start
  8.9 2.6 copy-start.1
  10.9 133.8 %copy-start.5 = (f32[1024]{0:T(1024)S(1)}, f32[1024]{0:T(1024)}, u32[]{:S(2)}) copy-start(f32[1024]{0:T(1024)} %param.14) | copy-start | bytes 12292
  72.4 191.4 %reduce-scatter.2.cloned.1.call-start = ((), (), s32[]{:S(2)}) async-start(), calls=%async_computation.2 | async-start | bytes 4718592 | tf_op jit(solution)/shard_map/reduce_scatter | solution.py:305
  162.0 4.0 %copy-start.2 = (f32[512,2,1024]{2,0,1:T(8,128)S(1)}, f32[512,2,1024]{2,0,1:T(8,128)}, u32[]{:S(2)}) copy-start(f32[512,2,1024]{2,0,1:T(8,128)} %get-tuple-element.7) | copy-start | bytes 12582916
Sparse Core Ops, SparseCore 0:
  72.5 72.1 all-gather.1
  177.3 86.4 reduce-scatter.1

commit v2 on v1

--- a/solution.py
+++ b/solution.py
@@ -189,6 +189,314 @@
     )(doc_lengths, packed, residual.transpose(1, 0, 2), norm_gain[None, :])
 
 
+def turn(z, step):
+    return (3 * (1 - lax.div(z, 2)), lax.rem(2 + 3 * z, 5), 1 + lax.rem(z, 2), z)[step]
+
+
+def head_kernel(
+    lengths_ref,
+    hidden_ref,
+    weight_hbm,
+    bias_ref,
+    pooled_ref,
+    grad_ref,
+    weight,
+    rows,
+    logits,
+    partials,
+    slopes,
+    across,
+    kept,
+    from_side,
+    from_line,
+    passing,
+    weight_sem,
+    own_sem,
+    row_send,
+    row_recv,
+    sum_send,
+    sum_recv,
+    side_send,
+    side_recv,
+    line_send,
+    line_recv,
+):
+    seq_at = lax.axis_index("seq")
+    vocab_at = lax.axis_index("vocab")
+    z, x = lax.div(vocab_at, 2), lax.rem(vocab_at, 2)
+    docs_count, tokens_here, width = grad_ref.shape
+    block_rows = docs_count * tokens_here
+    entries = weight.shape[1]
+    seq_count = partials.shape[0]
+    up, down, side = (seq_at, vocab_at + 2), (seq_at, vocab_at - 2), (seq_at, z * 2 + 1 - x)
+    mesh_id = pl.DeviceIdType.MESH
+
+    load = pltpu.make_async_copy(weight_hbm, weight, weight_sem)
+    load.start()
+    own = pltpu.make_async_copy(hidden_ref, rows.at[vocab_at], own_sem)
+    own.start()
+
+    barrier = pltpu.get_barrier_semaphore()
+    pl.semaphore_signal(barrier, inc=1, device_id=side, device_id_type=mesh_id)
+    for step in range(1, seq_count):
+        mate = (lax.rem(seq_at + step, seq_count), vocab_at)
+        pl.semaphore_signal(barrier, inc=1, device_id=mate, device_id_type=mesh_id)
+
+    @pl.when(z < 3)
+    def greet_up():
+        pl.semaphore_signal(barrier, inc=1, device_id=up, device_id_type=mesh_id)
+
+    @pl.when(z > 0)
+    def greet_down():
+        pl.semaphore_signal(barrier, inc=1, device_id=down, device_id_type=mesh_id)
+
+    pl.semaphore_wait(barrier, seq_count + lax.div(z + 3, 4) + lax.div(6 - z, 4))
+
+    def row_copy(slot, way):
+        return pltpu.make_async_remote_copy(
+            src_ref=rows.at[slot],
+            dst_ref=rows.at[slot],
+            send_sem=row_send.at[slot, way],
+            recv_sem=row_recv.at[slot],
+            device_id=(up, down, side)[way],
+            device_id_type=mesh_id,
+        )
+
+    def pass_rows(row, act):
+        slot = row * 2 + x
+
+        @pl.when(jnp.logical_and(row <= z, z < 3))
+        def upward():
+            act(row_copy(slot, 0))
+
+        @pl.when(jnp.logical_and(row >= z, z > 0))
+        def downward():
+            act(row_copy(slot, 1))
+
+        act(row_copy(slot, 2))
+
+    partials[seq_at] = jnp.zeros((docs_count, entries), jnp.float32)
+    tile = 256
+
+    def project(slot):
+        block = rows[slot]
+
+        @pl.loop(0, entries // tile)
+        def columns(step):
+            at = pl.ds(pl.multiple_of(step * tile, tile), tile)
+            found = (
+                jnp.dot(block, weight[:, at], preferred_element_type=jnp.float32)
+                + bias_ref[:, at]
+            )
+            first = (seq_at * 8 + slot) * tokens_here
+            place_of = first + lax.broadcasted_iota(jnp.int32, (tokens_here, tile), 0)
+            for doc in range(docs_count):
+                real = place_of < lengths_ref[doc]
+                part = found[doc * tokens_here : (doc + 1) * tokens_here]
+                base = 1.0 + jnp.maximum(part, 0.0)
+                power = base * base
+                power = power * power
+                boosted = jnp.where(real, power * power, 0.0)
+                total = jnp.sum(boosted, axis=0, keepdims=True)
+                partials[seq_at, doc : doc + 1, at] = (
+                    partials[seq_at, doc : doc + 1, at] + total
+                )
+                logits[slot, doc * tokens_here : (doc + 1) * tokens_here, at] = jnp.where(
+                    real, part, 0.0
+                )
+
+    own.wait()
+    pass_rows(z, lambda copy: copy.start())
+    load.wait()
+    project(vocab_at)
+    for step in range(1, 4):
+        row, before = turn(z, 3 - step), turn(z, 4 - step)
+        row_copy(row * 2 + x, 2).wait_recv()
+        pass_rows(row, lambda copy: copy.start())
+        project(row * 2 + x)
+        row_copy(before * 2 + 1 - x, 2).wait_recv()
+        project(before * 2 + 1 - x)
+    last = turn(z, 0) * 2 + 1 - x
+    row_copy(last, 2).wait_recv()
+    project(last)
+
+    def sum_copy(step, source):
+        return pltpu.make_async_remote_copy(
+            src_ref=partials.at[seq_at],
+            dst_ref=partials.at[source],
+            send_sem=sum_send.at[step],
+            recv_sem=sum_recv.at[source],
+            device_id=(lax.rem(seq_at + step, seq_count), vocab_at),
+            device_id_type=mesh_id,
+        )
+
+    for step in range(1, seq_count):
+        sum_copy(step, seq_at).start()
+    for step in range(1, seq_count):
+        sum_copy(step, lax.rem(seq_at + step, seq_count)).wait_recv()
+    totals = partials[0]
+    for other in range(1, seq_count):
+        totals = totals + partials[other]
+    usage = jnp.zeros((1, entries), jnp.float32)
+    for doc in range(docs_count):
+        length = jnp.full((1, entries), lengths_ref[doc], jnp.int32).astype(jnp.float32)
+        pooled = jnp.log(totals[doc : doc + 1] / length) / sharpness
+        pooled_ref[doc : doc + 1, :] = pooled
+        usage = usage + pooled
+    usage = usage / docs_count
+    coefficient = [
+        2.0 * flops_weight / docs_count * usage / totals[doc : doc + 1]
+        for doc in range(docs_count)
+    ]
+
+    def slope(slot):
+        for doc in range(docs_count):
+            part = logits[slot, doc * tokens_here : (doc + 1) * tokens_here]
+            base = 1.0 + jnp.maximum(part, 0.0)
+            square = base * base
+            boosted_slope = square * square * (square * base)
+            slopes[doc * tokens_here : (doc + 1) * tokens_here] = jnp.where(
+                part > 0.0, coefficient[doc] * boosted_slope, 0.0
+            ).astype(jnp.bfloat16)
+
+    def gradient(slot, write):
+        slope(slot)
+
+        @pl.loop(0, width // tile)
+        def features(step):
+            at = pl.ds(pl.multiple_of(step * tile, tile), tile)
+            write(
+                at,
+                lax.dot_general(
+                    slopes[...],
+                    weight[at, :],
+                    (((1,), (1,)), ((), ())),
+                    preferred_element_type=jnp.float32,
+                ),
+            )
+
+    def side_copy(row):
+        return pltpu.make_async_remote_copy(
+            src_ref=across.at[row],
+            dst_ref=from_side.at[row],
+            send_sem=side_send.at[row],
+            recv_sem=side_recv.at[row],
+            device_id=side,
+            device_id_type=mesh_id,
+        )
+
+    def line_copy(row, way):
+        return pltpu.make_async_remote_copy(
+            src_ref=passing.at[row],
+            dst_ref=from_line.at[way, row],
+            send_sem=line_send.at[row],
+            recv_sem=line_recv.at[way, row],
+            device_id=(up, down)[way],
+            device_id_type=mesh_id,
+        )
+
+    for step in range(4):
+        row = turn(z, step)
+
+        def write_across(at, value):
+            across[row, :, at] = value.astype(jnp.bfloat16)
+
+        gradient(row * 2 + 1 - x, write_across)
+        side_copy(row).start()
+
+    for step in range(4):
+        row = turn(z, step)
+
+        def write_kept(at, value):
+            kept[row, :, at] = value
+
+        gradient(row * 2 + x, write_kept)
+        side_copy(row).wait_recv()
+
+        @pl.when(jnp.logical_and(row >= z, z > 0))
+        def from_below():
+            line_copy(row, 0).wait_recv()
+            kept[row] = kept[row] + from_line[0, row].astype(jnp.float32)
+
+        @pl.when(jnp.logical_and(row <= z, z < 3))
+        def from_above():
+            line_copy(row, 1).wait_recv()
+            kept[row] = kept[row] + from_line[1, row].astype(jnp.float32)
+
+        total = (kept[row] + from_side[row].astype(jnp.float32)).astype(jnp.bfloat16)
+        if step < 3:
+            passing[row] = total
+
+            @pl.when(row > z)
+            def upward():
+                line_copy(row, 0).start()
+
+            @pl.when(row < z)
+            def downward():
+                line_copy(row, 1).start()
+
+        else:
+            grad_ref[...] = total.reshape(docs_count, tokens_here, width)
+
+    for step in range(4):
+        row = turn(z, step)
+        pass_rows(row, lambda copy: copy.wait_send())
+        side_copy(row).wait_send()
+        if step < 3:
+            line_copy(row, 0).wait_send()
+    for step in range(1, seq_count):
+        sum_copy(step, seq_at).wait_send()
+
+
+def head_all(hidden, head_weight, head_bias, doc_lengths):
+    docs_count, tokens_here, width = hidden.shape
+    entries = head_weight.shape[1]
+    block_rows = docs_count * tokens_here
+    vocab_count = lax.axis_size("vocab")
+    seq_count = lax.axis_size("seq")
+    vmem = pl.BlockSpec(memory_space=pltpu.VMEM)
+    dma = pltpu.SemaphoreType.DMA
+    return pl.pallas_call(
+        head_kernel,
+        out_shape=(
+            jax.ShapeDtypeStruct((docs_count, entries), jnp.float32),
+            jax.ShapeDtypeStruct((docs_count, tokens_here, width), jnp.bfloat16),
+        ),
+        in_specs=[
+            pl.BlockSpec(memory_space=pltpu.SMEM),
+            vmem,
+            pl.BlockSpec(memory_space=pl.ANY),
+            vmem,
+        ],
+        out_specs=(vmem, vmem),
+        scratch_shapes=[
+            pltpu.VMEM((width, entries), jnp.bfloat16),
+            pltpu.VMEM((vocab_count, block_rows, width), jnp.bfloat16),
+            pltpu.VMEM((vocab_count, block_rows, entries), jnp.float32),
+            pltpu.VMEM((seq_count, docs_count, entries), jnp.float32),
+            pltpu.VMEM((block_rows, entries), jnp.bfloat16),
+            pltpu.VMEM((4, block_rows, width), jnp.bfloat16),
+            pltpu.VMEM((4, block_rows, width), jnp.float32),
+            pltpu.VMEM((4, block_rows, width), jnp.bfloat16),
+            pltpu.VMEM((2, 4, block_rows, width), jnp.bfloat16),
+            pltpu.VMEM((4, block_rows, width), jnp.bfloat16),
+            dma,
+            dma,
+            dma((vocab_count, 3)),
+            dma((vocab_count,)),
+            dma((seq_count,)),
+            dma((seq_count,)),
+            dma((4,)),
+            dma((4,)),
+            dma((4,)),
+            dma((2, 4)),
+        ],
+        compiler_params=pltpu.CompilerParams(
+            collective_id=2, has_side_effects=True, vmem_limit_bytes=48 * 1024 * 1024
+        ),
+    )(doc_lengths, hidden.reshape(block_rows, width), head_weight, head_bias[None, :])
+
+
 def attend_blocks(
     queries, key_vectors, value_vectors, residual, norm_gain, doc_lengths
 ):
@@ -265,14 +573,16 @@
     docs_count = queries.shape[1]
     vocab_count = lax.axis_size("vocab")
     seq_at = lax.axis_index("seq")
-    if lax.axis_size("seq") * vocab_count == docs_count * (queries.shape[2] // HEAD_DIM):
+    heads = queries.shape[2] // HEAD_DIM
+    if vocab_count == 8 and lax.axis_size("seq") * vocab_count == docs_count * heads:
         hidden = attend_all(
             queries, key_vectors, value_vectors, residual, norm_gain, doc_lengths
-        ).transpose(1, 0, 2)
-    else:
-        hidden = attend_blocks(
-            queries, key_vectors, value_vectors, residual, norm_gain, doc_lengths
-        )
+        )
+        pooled, gradient = head_all(hidden, head_weight, head_bias, doc_lengths)
+        return (pooled, gradient.transpose(1, 0, 2))
+    hidden = attend_blocks(
+        queries, key_vectors, value_vectors, residual, norm_gain, doc_lengths
+    )
     arrived = lax.all_gather(hidden, "vocab", axis=0, tiled=True)
     row_count = arrived.shape[0]
     flattened = jnp.dot(

time: 273 us -> 182 us (0.67)
  waiting for transfers between devices: 159 us -> 0 us
  Pallas kernels: 60.9 us -> 173 us
  matrix products: 22.5 us -> 0 us
  between operations: 14.2 us -> 0.79 us
  blocking collectives: 5.92 us -> 0 us
  other arithmetic: 4.22 us -> 0.17 us
    pallas_call x0 -> x1, Pallas kernels: none -> 113 us  [head_all(): pl.pallas_call(head_kernel, out_shape=(jax.ShapeDtypeStruct((docs_count,...]
    reduce_scatter x1 -> x0, waiting for transfers between devices: 86.6 us -> none  [local(): lax.psum_scatter(flattened.reshape(gathered_rows, docs_count, head_weight...]
    all_gather x1 -> x0, waiting for transfers between devices: 72.1 us -> none  [local(): arrived = lax.all_gather(hidden, 'vocab', axis=0, tiled=True)]
    dot_general x2 -> x0, matrix products: 22.5 us -> none  [the longest x1 11.4 us: local(): jnp.dot(arrived.reshape(row_count * docs_count, arrived.shape[2]), head_w...]
    psum x1 -> x0, blocking collectives: 5.92 us -> none  [local(): totals = lax.psum(partial_sums, 'seq')]
    unnamed x1 -> x0, other arithmetic: 3.26 us -> none
  transfers between devices with their start and end apart: 2 -> 0, of which waited for: 2 -> 0; matrix products, arithmetic and copies ran while one was open for 0% -> 0% of each run, Pallas kernels for 0% -> 0%
where the time goes in v2:
time: 182 us; the launch traced here: 180 us
  Pallas kernels  173 us (95%)
  local copies, waits for them, and re-layouts  5.7 us (3%)
    pallas_call x1, Pallas kernels, head_all(): pl.pallas_call(head_kernel, out_shape=(jax.ShapeDtypeStruct((docs_count,...  113 us
    pallas_call x1, Pallas kernels, attend_all(): pl.pallas_call(functools.partial(attend_kernel, devices, vocab_count, hea...  60.1 us

profile of v2, /device:TPU:0, one launch (start us, length us, event | category | flops | bytes accessed | tf_op | source)
XLA Modules:
  0.0 179.7 jit_solution(7818945062777319069)
XLA Ops:
  0.6 0.0 copy-start.4
  0.6 1.4 stack.12
  2.1 0.0 copy-start.5
  2.1 0.2 copy.10
  2.3 0.0 copy-done.4
  2.3 0.3 stack.13
  2.6 0.2 copy.11
  2.9 0.3 copy-done.5
  3.1 0.3 stack.14
  3.5 0.0 copy-start.6
  3.5 0.0 copy-start.1
  3.5 0.2 copy.12
  3.7 0.0 copy-start.3
  3.7 0.0 copy-start
  3.7 0.2 pad_maximum_fusion
  3.9 0.6 copy-done.6
  4.5 0.2 copy.16
  4.7 0.0 copy-start.2
  4.7 0.0 copy-done.1
  4.7 0.0 copy-done.3
  4.7 60.1 %shard_map.95 = bf16[2,64,2048]{2,1,0:T(8,128)(2,1)S(1)} custom-call(s32[2]{0:T(128)S(1)} %copy-done.3, bf16[32,3,64,128]{3,2,1,0:T(8,128)(2,1)S(1)} %bitcast.10, bf16[2,64,2048]{2,1,0:T(8,128)(2,1)S(1)} %bitcast.11, f32[1,2048]{1,0:T(1,128)S(1)} %bitcast.14), custom_call_target="tpu_custom_call" | custom-call | tf_op jit(solution)/shard_map/pallas_call | solution.py:171
  64.8 0.0 copy-done
  64.8 0.0 copy-done.2
  64.8 113.0 %shard_map.96 = (f32[2,1024]{1,0:T(2,128)S(1)}, bf16[2,64,2048]{2,1,0:T(8,128)(2,1)S(1)}) custom-call(s32[2]{0:T(128)S(1)} %copy-done.3, bf16[128,2048]{1,0:T(8,128)(2,1)S(1)} %bitcast.12, bf16[2048,1024]{1,0:T(8,128)(2,1)S(1)} %copy-done, f32[1,1024]{1,0:T(1,128)S(1)} %bitcast.15), custom_call_target="tpu_custom_call" | custom-call | tf_op jit(solution)/shard_map/pallas_call | solution.py:459
  177.8 1.3 copy.14
  179.1 0.6 copy.18
Async XLA Ops:
  0.6 1.7 copy-start.4
  2.1 1.0 copy-start.5
  3.5 1.0 copy-start.6
  3.5 1.2 copy-start.1
  3.7 1.0 copy-start.3
  3.7 61.1 %copy-start = (bf16[2048,1024]{1,0:T(8,128)(2,1)S(1)}, bf16[2048,1024]{1,0:T(8,128)(2,1)}, u32[]{:S(2)}) copy-start(bf16[2048,1024]{1,0:T(8,128)(2,1)} %weight_hbm.1) | copy-start | bytes 12582916
  4.7 60.1 %copy-start.2 = (f32[1024]{0:T(1024)S(1)}, f32[1024]{0:T(1024)}, u32[]{:S(2)}) copy-start(f32[1024]{0:T(1024)} %param.14) | copy-start | bytes 12292

commit v3 on v2

--- a/solution.py
+++ b/solution.py
@@ -210,6 +210,7 @@
     from_side,
     from_line,
     passing,
+    from_partner,
     weight_sem,
     own_sem,
     row_send,
@@ -220,6 +221,8 @@
     side_recv,
     line_send,
     line_recv,
+    partner_send,
+    partner_recv,
 ):
     seq_at = lax.axis_index("seq")
     vocab_at = lax.axis_index("vocab")
@@ -229,6 +232,8 @@
     entries = weight.shape[1]
     seq_count = partials.shape[0]
     up, down, side = (seq_at, vocab_at + 2), (seq_at, vocab_at - 2), (seq_at, z * 2 + 1 - x)
+    partner_row = z + 1 - 2 * lax.rem(z, 2)
+    partner = (seq_at, partner_row * 2 + x)
     mesh_id = pl.DeviceIdType.MESH
 
     load = pltpu.make_async_copy(weight_hbm, weight, weight_sem)
@@ -252,28 +257,35 @@
 
     pl.semaphore_wait(barrier, seq_count + lax.div(z + 3, 4) + lax.div(6 - z, 4))
 
-    def row_copy(slot, way):
+    def row_copy(slot, way, half):
+        part = rows.at[slot, pl.ds(half * tokens_here, tokens_here)]
         return pltpu.make_async_remote_copy(
-            src_ref=rows.at[slot],
-            dst_ref=rows.at[slot],
-            send_sem=row_send.at[slot, way],
-            recv_sem=row_recv.at[slot],
-            device_id=(up, down, side)[way],
+            src_ref=part,
+            dst_ref=part,
+            send_sem=row_send.at[slot, way, half],
+            recv_sem=row_recv.at[slot, half],
+            device_id=(up, down, side, partner)[way],
             device_id_type=mesh_id,
         )
 
-    def pass_rows(row, act):
+    def pass_rows(row, half, act):
         slot = row * 2 + x
 
         @pl.when(jnp.logical_and(row <= z, z < 3))
         def upward():
-            act(row_copy(slot, 0))
+            act(row_copy(slot, 0, half))
 
         @pl.when(jnp.logical_and(row >= z, z > 0))
         def downward():
-            act(row_copy(slot, 1))
-
-        act(row_copy(slot, 2))
+            act(row_copy(slot, 1, half))
+
+        if half == 0:
+            act(row_copy(slot, 2, half))
+        else:
+
+            @pl.when(row != partner_row)
+            def sideways():
+                act(row_copy(slot, 2, half))
 
     partials[seq_at] = jnp.zeros((docs_count, entries), jnp.float32)
     tile = 256
@@ -306,18 +318,26 @@
                 )
 
     own.wait()
-    pass_rows(z, lambda copy: copy.start())
+    for half in range(2):
+        pass_rows(z, half, lambda copy: copy.start())
     load.wait()
     project(vocab_at)
     for step in range(1, 4):
         row, before = turn(z, 3 - step), turn(z, 4 - step)
-        row_copy(row * 2 + x, 2).wait_recv()
-        pass_rows(row, lambda copy: copy.start())
-        project(row * 2 + x)
-        row_copy(before * 2 + 1 - x, 2).wait_recv()
+        for half in range(2):
+            row_copy(row * 2 + x, 2, half).wait_recv()
+            pass_rows(row, half, lambda copy: copy.start())
+        if step > 1:
+            project(row * 2 + x)
+        for half in range(2):
+            row_copy(before * 2 + 1 - x, 2, half).wait_recv()
+        if step == 1:
+            row_copy(before * 2 + 1 - x, 3, 1).start()
+            project(row * 2 + x)
         project(before * 2 + 1 - x)
     last = turn(z, 0) * 2 + 1 - x
-    row_copy(last, 2).wait_recv()
+    for half in range(2):
+        row_copy(last, 2, half).wait_recv()
     project(last)
 
     def sum_copy(step, source):
@@ -375,22 +395,33 @@
                 ),
             )
 
-    def side_copy(row):
+    def side_copy(row, half):
+        part = pl.ds(half * tokens_here, tokens_here)
         return pltpu.make_async_remote_copy(
-            src_ref=across.at[row],
-            dst_ref=from_side.at[row],
-            send_sem=side_send.at[row],
-            recv_sem=side_recv.at[row],
+            src_ref=across.at[row, part],
+            dst_ref=from_side.at[row, part],
+            send_sem=side_send.at[row, half],
+            recv_sem=side_recv.at[row, half],
             device_id=side,
             device_id_type=mesh_id,
         )
 
-    def line_copy(row, way):
+    partner_copy = pltpu.make_async_remote_copy(
+        src_ref=across.at[partner_row, pl.ds(tokens_here, tokens_here)],
+        dst_ref=from_partner,
+        send_sem=partner_send,
+        recv_sem=partner_recv,
+        device_id=partner,
+        device_id_type=mesh_id,
+    )
+
+    def line_copy(row, way, half):
+        part = pl.ds(half * tokens_here, tokens_here)
         return pltpu.make_async_remote_copy(
-            src_ref=passing.at[row],
-            dst_ref=from_line.at[way, row],
-            send_sem=line_send.at[row],
-            recv_sem=line_recv.at[way, row],
+            src_ref=passing.at[row, part],
+            dst_ref=from_line.at[way, row, part],
+            send_sem=line_send.at[row, half],
+            recv_sem=line_recv.at[way, row, half],
             device_id=(up, down)[way],
             device_id_type=mesh_id,
         )
@@ -402,7 +433,16 @@
             across[row, :, at] = value.astype(jnp.bfloat16)
 
         gradient(row * 2 + 1 - x, write_across)
-        side_copy(row).start()
+        side_copy(row, 0).start()
+        if step < 3:
+
+            @pl.when(row == partner_row)
+            def by_line():
+                partner_copy.start()
+
+            @pl.when(row != partner_row)
+            def by_side():
+                side_copy(row, 1).start()
 
     for step in range(4):
         row = turn(z, step)
@@ -411,39 +451,67 @@
             kept[row, :, at] = value
 
         gradient(row * 2 + x, write_kept)
-        side_copy(row).wait_recv()
-
-        @pl.when(jnp.logical_and(row >= z, z > 0))
-        def from_below():
-            line_copy(row, 0).wait_recv()
-            kept[row] = kept[row] + from_line[0, row].astype(jnp.float32)
-
-        @pl.when(jnp.logical_and(row <= z, z < 3))
-        def from_above():
-            line_copy(row, 1).wait_recv()
-            kept[row] = kept[row] + from_line[1, row].astype(jnp.float32)
-
-        total = (kept[row] + from_side[row].astype(jnp.float32)).astype(jnp.bfloat16)
-        if step < 3:
-            passing[row] = total
-
-            @pl.when(row > z)
-            def upward():
-                line_copy(row, 0).start()
-
-            @pl.when(row < z)
-            def downward():
-                line_copy(row, 1).start()
-
-        else:
-            grad_ref[...] = total.reshape(docs_count, tokens_here, width)
+        if step == 0:
+            partner_copy.wait_recv()
+            late = pl.ds(tokens_here, tokens_here)
+            across[z, late] = (
+                across[z, late].astype(jnp.float32) + from_partner[...].astype(jnp.float32)
+            ).astype(jnp.bfloat16)
+            side_copy(z, 1).start()
+        for half in range(2):
+            part = pl.ds(half * tokens_here, tokens_here)
+
+            @pl.when(jnp.logical_and(row >= z, z > 0))
+            def from_below():
+                line_copy(row, 0, half).wait_recv()
+                kept[row, part] = kept[row, part] + from_line[0, row, part].astype(
+                    jnp.float32
+                )
+
+            @pl.when(jnp.logical_and(row <= z, z < 3))
+            def from_above():
+                line_copy(row, 1, half).wait_recv()
+                kept[row, part] = kept[row, part] + from_line[1, row, part].astype(
+                    jnp.float32
+                )
+
+            def add_side():
+                side_copy(row, half).wait_recv()
+                kept[row, part] = kept[row, part] + from_side[row, part].astype(jnp.float32)
+
+            if half == 0 or step == 3:
+                add_side()
+            else:
+                pl.when(row != partner_row)(add_side)
+            total = kept[row, part].astype(jnp.bfloat16)
+            if step < 3:
+                passing[row, part] = total
+
+                @pl.when(row > z)
+                def upward():
+                    line_copy(row, 0, half).start()
+
+                @pl.when(row < z)
+                def downward():
+                    line_copy(row, 1, half).start()
+
+            else:
+                grad_ref[half] = total
 
     for step in range(4):
         row = turn(z, step)
-        pass_rows(row, lambda copy: copy.wait_send())
-        side_copy(row).wait_send()
-        if step < 3:
-            line_copy(row, 0).wait_send()
+        for half in range(2):
+            pass_rows(row, half, lambda copy: copy.wait_send())
+            if step < 3:
+                line_copy(row, 0, half).wait_send()
+        side_copy(row, 0).wait_send()
+
+        @pl.when(row != partner_row)
+        def sent():
+            side_copy(row, 1).wait_send()
+
+    partner_copy.wait_send()
+    row_copy(z * 2 + 1 - x, 3, 1).wait_send()
     for step in range(1, seq_count):
         sum_copy(step, seq_at).wait_send()
 
@@ -480,16 +548,19 @@
             pltpu.VMEM((4, block_rows, width), jnp.bfloat16),
             pltpu.VMEM((2, 4, block_rows, width), jnp.bfloat16),
             pltpu.VMEM((4, block_rows, width), jnp.bfloat16),
+            pltpu.VMEM((tokens_here, width), jnp.bfloat16),
             dma,
             dma,
-            dma((vocab_count, 3)),
-            dma((vocab_count,)),
+            dma((vocab_count, 4, 2)),
+            dma((vocab_count, 2)),
             dma((seq_count,)),
             dma((seq_count,)),
-            dma((4,)),
-            dma((4,)),
-            dma((4,)),
-            dma((2, 4)),
+            dma((4, 2)),
+            dma((4, 2)),
+            dma((4, 2)),
+            dma((2, 4, 2)),
+            dma,
+            dma,
         ],
         compiler_params=pltpu.CompilerParams(
             collective_id=2, has_side_effects=True, vmem_limit_bytes=48 * 1024 * 1024

time: 182 us -> 171 us (0.940)
  Pallas kernels: 173 us -> 164 us
    pallas_call x1, Pallas kernels: 113 us -> 104 us  [head_all(): pl.pallas_call(head_kernel, out_shape=(jax.ShapeDtypeStruct((docs_count,...]
where the time goes in v3:
time: 171 us; the launch traced here: 170 us
  Pallas kernels  164 us (96%)
  local copies, waits for them, and re-layouts  5.7 us (3%)
    pallas_call x1, Pallas kernels, head_all(): pl.pallas_call(head_kernel, out_shape=(jax.ShapeDtypeStruct((docs_count,...  104 us
    pallas_call x1, Pallas kernels, attend_all(): pl.pallas_call(functools.partial(attend_kernel, devices, vocab_count, hea...  60.1 us

profile of v3, /device:TPU:0, one launch (start us, length us, event | category | flops | bytes accessed | tf_op | source)
XLA Modules:
  0.0 170.5 jit_solution(16492009840694884791)
XLA Ops:
  0.6 0.0 copy-start.4
  0.6 1.4 stack.12
  2.1 0.0 copy-start.5
  2.1 0.2 copy.10
  2.3 0.0 copy-done.4
  2.3 0.3 stack.13
  2.6 0.2 copy.11
  2.9 0.3 copy-done.5
  3.1 0.3 stack.14
  3.5 0.0 copy-start.6
  3.5 0.0 copy-start.1
  3.5 0.2 copy.12
  3.7 0.0 copy-start.3
  3.7 0.0 copy-start
  3.7 0.2 pad_maximum_fusion
  3.9 0.6 copy-done.6
  4.5 0.2 copy.16
  4.7 0.0 copy-start.2
  4.7 0.0 copy-done.1
  4.7 0.0 copy-done.3
  4.7 60.1 %shard_map.95 = bf16[2,64,2048]{2,1,0:T(8,128)(2,1)S(1)} custom-call(s32[2]{0:T(128)S(1)} %copy-done.3, bf16[32,3,64,128]{3,2,1,0:T(8,128)(2,1)S(1)} %bitcast.10, bf16[2,64,2048]{2,1,0:T(8,128)(2,1)S(1)} %bitcast.11, f32[1,2048]{1,0:T(1,128)S(1)} %bitcast.14), custom_call_target="tpu_custom_call" | custom-call | tf_op jit(solution)/shard_map/pallas_call | solution.py:171
  64.8 0.0 copy-done
  64.8 0.0 copy-done.2
  64.8 103.7 %shard_map.96 = (f32[2,1024]{1,0:T(2,128)S(1)}, bf16[2,64,2048]{2,1,0:T(8,128)(2,1)S(1)}) custom-call(s32[2]{0:T(128)S(1)} %copy-done.3, bf16[128,2048]{1,0:T(8,128)(2,1)S(1)} %bitcast.12, bf16[2048,1024]{1,0:T(8,128)(2,1)S(1)} %copy-done, f32[1,1024]{1,0:T(1,128)S(1)} %bitcast.15), custom_call_target="tpu_custom_call" | custom-call | tf_op jit(solution)/shard_map/pallas_call | solution.py:527
  168.5 1.3 copy.14
  169.9 0.6 copy.18
Async XLA Ops:
  0.6 1.7 copy-start.4
  2.1 1.0 copy-start.5
  3.5 1.0 copy-start.6
  3.5 1.2 copy-start.1
  3.7 1.0 copy-start.3
  3.7 61.1 %copy-start = (bf16[2048,1024]{1,0:T(8,128)(2,1)S(1)}, bf16[2048,1024]{1,0:T(8,128)(2,1)}, u32[]{:S(2)}) copy-start(bf16[2048,1024]{1,0:T(8,128)(2,1)} %weight_hbm.1) | copy-start | bytes 12582916
  4.7 60.1 %copy-start.2 = (f32[1024]{0:T(1024)S(1)}, f32[1024]{0:T(1024)}, u32[]{:S(2)}) copy-start(f32[1024]{0:T(1024)} %param.14) | copy-start | bytes 12292

commit v4 on v3

--- a/solution.py
+++ b/solution.py
@@ -290,8 +290,9 @@
     partials[seq_at] = jnp.zeros((docs_count, entries), jnp.float32)
     tile = 256
 
-    def project(slot):
-        block = rows[slot]
+    def project(slot, docs=range(docs_count)):
+        low = docs[0] * tokens_here
+        block = rows[slot, low : low + len(docs) * tokens_here]
 
         @pl.loop(0, entries // tile)
         def columns(step):
@@ -302,9 +303,9 @@
             )
             first = (seq_at * 8 + slot) * tokens_here
             place_of = first + lax.broadcasted_iota(jnp.int32, (tokens_here, tile), 0)
-            for doc in range(docs_count):
+            for doc in docs:
                 real = place_of < lengths_ref[doc]
-                part = found[doc * tokens_here : (doc + 1) * tokens_here]
+                part = found[doc * tokens_here - low : (doc + 1) * tokens_here - low]
                 base = 1.0 + jnp.maximum(part, 0.0)
                 power = base * base
                 power = power * power
@@ -338,7 +339,7 @@
     last = turn(z, 0) * 2 + 1 - x
     for half in range(2):
         row_copy(last, 2, half).wait_recv()
-    project(last)
+        project(last, range(half, half + 1))
 
     def sum_copy(step, source):
         return pltpu.make_async_remote_copy(

time: 171 us -> 170 us (level)
  no operation moved by 1% of the time
where the time goes in v4:
time: 170 us
  Pallas kernels  164 us (96%)
  local copies, waits for them, and re-layouts  5.7 us (3%)
    pallas_call x1, Pallas kernels, head_all(): pl.pallas_call(head_kernel, out_shape=(jax.ShapeDtypeStruct((docs_count,...  104 us
    pallas_call x1, Pallas kernels, attend_all(): pl.pallas_call(functools.partial(attend_kernel, devices, vocab_count, hea...  60.1 us

profile of v4, /device:TPU:0, one launch (start us, length us, event | category | flops | bytes accessed | tf_op | source)
XLA Modules:
  0.0 170.3 jit_solution(15971817924560635743)
XLA Ops:
  0.6 0.0 copy-start.4
  0.6 1.4 stack.12
  2.1 0.0 copy-start.5
  2.1 0.2 copy.10
  2.3 0.0 copy-done.4
  2.3 0.3 stack.13
  2.6 0.2 copy.11
  2.9 0.3 copy-done.5
  3.1 0.3 stack.14
  3.5 0.0 copy-start.6
  3.5 0.0 copy-start.1
  3.5 0.2 copy.12
  3.7 0.0 copy-start.3
  3.7 0.0 copy-start
  3.7 0.2 pad_maximum_fusion
  3.9 0.6 copy-done.6
  4.5 0.2 copy.16
  4.7 0.0 copy-start.2
  4.7 0.0 copy-done.1
  4.7 0.0 copy-done.3
  4.7 60.1 %shard_map.95 = bf16[2,64,2048]{2,1,0:T(8,128)(2,1)S(1)} custom-call(s32[2]{0:T(128)S(1)} %copy-done.3, bf16[32,3,64,128]{3,2,1,0:T(8,128)(2,1)S(1)} %bitcast.10, bf16[2,64,2048]{2,1,0:T(8,128)(2,1)S(1)} %bitcast.11, f32[1,2048]{1,0:T(1,128)S(1)} %bitcast.14), custom_call_target="tpu_custom_call" | custom-call | tf_op jit(solution)/shard_map/pallas_call | solution.py:171
  64.8 0.0 copy-done
  64.8 0.0 copy-done.2
  64.8 103.6 %shard_map.96 = (f32[2,1024]{1,0:T(2,128)S(1)}, bf16[2,64,2048]{2,1,0:T(8,128)(2,1)S(1)}) custom-call(s32[2]{0:T(128)S(1)} %copy-done.3, bf16[128,2048]{1,0:T(8,128)(2,1)S(1)} %bitcast.12, bf16[2048,1024]{1,0:T(8,128)(2,1)S(1)} %copy-done, f32[1,1024]{1,0:T(1,128)S(1)} %bitcast.15), custom_call_target="tpu_custom_call" | custom-call | tf_op jit(solution)/shard_map/pallas_call | solution.py:528
  168.4 1.3 copy.14
  169.7 0.6 copy.18
Async XLA Ops:
  0.6 1.7 copy-start.4
  2.1 1.0 copy-start.5
  3.5 1.0 copy-start.6
  3.5 1.2 copy-start.1
  3.7 1.0 copy-start.3
  3.7 61.1 %copy-start = (bf16[2048,1024]{1,0:T(8,128)(2,1)S(1)}, bf16[2048,1024]{1,0:T(8,128)(2,1)}, u32[]{:S(2)}) copy-start(bf16[2048,1024]{1,0:T(8,128)(2,1)} %weight_hbm.1) | copy-start | bytes 12582916
  4.7 60.1 %copy-start.2 = (f32[1024]{0:T(1024)S(1)}, f32[1024]{0:T(1024)}, u32[]{:S(2)}) copy-start(f32[1024]{0:T(1024)} %param.14) | copy-start | bytes 12292
